TPU v7x, 32 devices: a whole 2x2x4 slice. The times are simulated.
32 devices in a mesh: base: 16 (over z, y, x), facet: 2 (over core).
Axes of the slice: x: 2, y: 2, z: 4, core: 2. Of those that a mesh axis runs over, the one named last changes fastest.
Arguments:
- observed: float32 [2, 4, 64, 4096], P(None, None, None, 'base'), may hold values from -6 to 6
- station_pairs: int32 [2, 4096], P(None, 'base'), may hold values from 0 to 511, as said below
- station_uvw: float32 [4, 3, 512], replicated, may hold values from -40 to 40
- directions: float32 [2, 2, 256], P('facet'), may hold values from -0.3 to 0.3
- fluxes: float32 [2, 256], P('facet'), may hold values from 0.02 to 0.2
- counts: int32 [2], P('facet'), may hold values from 32 to 256, as said below
- jones_gains: float32 [2, 4, 2, 512], P(None, None, 'facet'), may hold values from -2 to 3
Outputs:
- residual: float32 [2, 4, 64, 4096], P(None, None, None, ('base', 'facet'))
- scaled_grad: float32 [2, 4, 2, 512], P(None, None, 'facet')
Inputs may be any that keep to these rules, and one draw needn't show every extreme that they name: `station_pairs`: the two stations of a baseline differ. `counts`: some facet holds exactly 256 live components and some other facet fewer.
All inputs are finite; a program needn't handle non-finite values.
Results may differ from a plain program's by a relative error of at most 0.0003.
Values sent between devices are 32-bit elements; how exact they have to be, the bound alone decides.
A program may use at most 64 MiB of HBM per device.

v0:
```python
import functools
import math

import jax
import jax.numpy as jnp
from jax import lax
from jax.experimental import pallas as pl
from jax.experimental.pallas import tpu as pltpu
from jax.sharding import PartitionSpec as P

MESH = pl.DeviceIdType.MESH
LANES = 128
TIMES = 4
CHANNELS = 16
ROWS = 9
STEP = 16
VMEM = pltpu.MemorySpace.VMEM
SMEM = pltpu.MemorySpace.SMEM

SIN = (4.442882919124344, -7.308245686509057, 3.6063542184328345, -0.846111650373896, 0.10982451642611356)
COS = (1.4142134962552284, -6.978850948563788, 5.73946037690675, -1.8835579059841707, 0.3106880275217573)


def poly(x, coefficients):
    value = coefficients[-1]
    for c in coefficients[-2::-1]:
        value = value * x + c
    return value


def cos_sin_turns(turns):
    magic = 12582912.0
    r = turns - ((turns + magic) - magic)
    x = r * r
    half_sin = r * poly(x, SIN)
    half_cos = poly(x, COS)
    return 1.0 - half_sin * half_sin, half_sin * half_cos


def split3(a):
    high = a.astype(jnp.bfloat16)
    rest = a - high.astype(jnp.float32)
    mid = rest.astype(jnp.bfloat16)
    low = (rest - mid.astype(jnp.float32)).astype(jnp.bfloat16)
    return high, mid, low


def exact_dot(a, hot, dims):
    out = None
    for part in split3(a):
        term = lax.dot_general(part, hot, (dims, ((), ())), preferred_element_type=jnp.float32)
        out = term if out is None else out + term
    return out


def product(a, b):
    out = []
    for i in range(2):
        for j in range(2):
            re = im = None
            for k in range(2):
                (x, y), (u, v) = a[2 * i + k], b[2 * k + j]
                r, s = x * u - y * v, x * v + y * u
                re, im = (r, s) if re is None else (re + r, im + s)
            out.append((re, im))
    return out


def adjoint(a):
    return [(a[i][0], -a[i][1]) for i in (0, 2, 1, 3)]


def radices(blocks):
    out = []
    while blocks > 1:
        out.append(4 if blocks % 4 == 0 else blocks)
        blocks //= out[-1]
    return out


def partners(blocks, facets):
    b = lax.axis_index("base")
    f = lax.axis_index("facet")
    phases = []
    stride = 1
    for radix in radices(blocks):
        digit = lax.rem(b // stride, radix)
        low = b - digit * stride
        turns = facets if stride == 1 else 1
        phases.append([(low + lax.rem(digit + d, radix) * stride, lax.rem(f + e, facets))
                       for d in range(radix) for e in range(turns) if d + e > 0])
        stride *= radix
    return phases


def message_counts(blocks, facets):
    return [r * (facets if i == 0 else 1) - 1 for i, r in enumerate(radices(blocks))]


def calibrate_kernel(blocks, facets, sliced, observed_ref, pairs_ref, uvw_ref, directions_ref, fluxes_ref, counts_ref,
                     gains_ref, out_ref, totals_ref, params, table, gathered, hot, base, angle, model, left, parts, mine,
                     *refs):
    phases = partners(blocks, facets)
    inboxes = refs[: len(phases)]
    copy_sem, params_send, params_recv, send_sem, recv_sem = refs[len(phases) :]
    me = lax.axis_index("facet")
    block = lax.axis_index("base")
    barrier = pltpu.get_barrier_semaphore()
    for phase in phases:
        for peer in phase:
            pl.semaphore_signal(barrier, inc=1, device_id=peer, device_id_type=MESH)
    width = out_ref.shape[3]
    stations = uvw_ref.shape[2]
    groups = stations // LANES
    cap = fluxes_ref.shape[1]
    start = pl.multiple_of(me * width, LANES)
    source = observed_ref.at[:, :, :, pl.ds(start, width)] if sliced else observed_ref
    copy = pltpu.make_async_copy(source, out_ref, copy_sem)
    copy.start()
    for i in range(2):
        for j in range(4):
            params[me, 4 * i + j : 4 * i + j + 1, :] = gains_ref[i, j]
    params[me, 8:16, :] = jnp.zeros((8, stations), jnp.float32)
    l = directions_ref[0, 0:1, :]
    m = directions_ref[0, 1:2, :]
    slots = lax.broadcasted_iota(jnp.int32, (1, cap), 1)
    params[me, 8:9, 0:cap] = l
    params[me, 9:10, 0:cap] = m
    params[me, 10:11, 0:cap] = jnp.sqrt(1.0 - l * l - m * m) - 1.0
    params[me, 11:12, 0:cap] = jnp.where(slots < counts_ref[0], fluxes_ref[...], 0.0)
    pairs = pairs_ref[:, pl.ds(start, width)] if sliced else pairs_ref[...]
    column = lax.broadcasted_iota(jnp.int32, (stations, width), 0)
    for side in range(2):
        hot[side] = (column == pairs[side : side + 1, :]).astype(jnp.float32).astype(jnp.bfloat16)
    pl.semaphore_wait(barrier, sum(message_counts(blocks, facets)))
    shares = []
    for d in range(1, facets):
        share = pltpu.make_async_remote_copy(
            src_ref=params.at[me], dst_ref=params.at[me], send_sem=params_send.at[d - 1],
            recv_sem=params_recv.at[d - 1], device_id=(block, lax.rem(me + d, facets)), device_id_type=MESH)
        share.start()
        shares.append(share)
    for t in range(TIMES):
        for axis in range(3):
            table[8 * t + axis : 8 * t + axis + 1, :] = uvw_ref[axis, t : t + 1, :]
        table[8 * t + 3 : 8 * t + 8, :] = jnp.zeros((5, stations), jnp.float32)
    table[32:40, :] = params[me, 0:8, :]
    own = pl.ds(pl.multiple_of(32 + 8 * me, 8), 8)
    for side in range(2):
        found = exact_dot(table[...], hot[side], ((1,), (0,)))
        gathered[side, 0:32, :] = found[0:32]
        gathered[side, own, :] = found[32:40]
    for t in range(TIMES):
        base[:, t * width : (t + 1) * width] = gathered[0, 8 * t : 8 * t + 8, :] - gathered[1, 8 * t : 8 * t + 8, :]
    row = lax.broadcasted_iota(jnp.int32, (8, width), 0)
    base[:, TIMES * width :] = (row == 3).astype(jnp.float32)

    def jones(k, side):
        rows = gathered[side, pl.ds(pl.multiple_of(32 + 8 * k, 8), 8), :]
        return [(rows[e : e + 1, :], rows[4 + e : 5 + e, :]) for e in range(4)]

    def facet_model(d, carry):
        k = lax.rem(me + d, facets)
        slots = jnp.transpose(params[k, 8:16, 0:cap])
        angle[...] = jnp.dot(slots, base[...], precision=lax.Precision.HIGHEST, preferred_element_type=jnp.float32)
        for t in range(TIMES):

            def step(i, acc):
                rows = pl.ds(pl.multiple_of(i * STEP, STEP), STEP)
                turns = angle[rows, t * width : (t + 1) * width]
                live = angle[rows, TIMES * width :]
                cz, sz = cos_sin_turns(turns * (79.0 / 64.0))
                c0, s0 = cos_sin_turns(turns * (1.0 / 64.0))
                cz, sz = cz * live, sz * live
                twice = 4.0 * (c0 * c0) - 2.0
                cs, ss = [c0, (twice - 1.0) * c0], [s0, (twice + 1.0) * s0]
                for j in range(2):
                    cs.append(twice * cs[-1] - cs[-2])
                    ss.append(twice * ss[-1] - ss[-2])
                c4 = cs[3] * c0 - ss[3] * s0
                s4 = ss[3] * c0 + cs[3] * s0
                cc, sn, sc, cn = cz * c4, sz * s4, sz * c4, cz * s4
                centres = ((cc + sn, sc - cn), (cc - sn, sc + cn))
                out = []
                for a, b in centres:
                    for j in range(4):
                        for value in (a * cs[j], b * ss[j], a * ss[j], b * cs[j]):
                            out.append(acc[len(out)] + (value[0:8] + value[8:16]))
                return tuple(out)

            zero = jnp.zeros((8, width), jnp.float32)
            acc = lax.fori_loop(0, cap // STEP, step, (zero,) * 32)
            real, imaginary = [None] * CHANNELS, [None] * CHANNELS
            for centre in range(2):
                for j in range(4):
                    p = acc[16 * centre + 4 * j : 16 * centre + 4 * j + 4]
                    up, down = 8 * centre + 4 + j, 8 * centre + 3 - j
                    real[up], real[down] = p[0] - p[1], p[0] + p[1]
                    imaginary[up], imaginary[down] = -(p[2] + p[3]), p[2] - p[3]
            for part, values in enumerate((real, imaginary)):
                sums = [jnp.sum(v, axis=0, keepdims=True) for v in values]
                model[k, part, CHANNELS * t : CHANNELS * (t + 1), :] = jnp.concatenate(sums, axis=0)
        return carry

    facet_model(0, 0)
    for d, share in enumerate(shares, 1):
        other = lax.rem(me + facets - d, facets)
        pltpu.make_async_copy(params.at[other], params.at[other], params_recv.at[d - 1]).wait()
        rows = pl.ds(pl.multiple_of(32 + 8 * other, 8), 8)
        for side in range(2):
            gathered[side, rows, :] = exact_dot(params[other, 0:8, :], hot[side], ((1,), (0,)))
    lax.fori_loop(1, facets, facet_model, 0)
    copy.wait()

    def subtract(k, carry):
        prod = product(jones(k, 0), adjoint(jones(k, 1)))
        re, im = model[k, 0], model[k, 1]
        for e, (x, y) in enumerate(prod):
            out_ref[0, e] = out_ref[0, e] - (re * x - im * y)
            out_ref[1, e] = out_ref[1, e] - (re * y + im * x)
        return carry

    lax.fori_loop(0, facets, subtract, 0)

    def terms(k, carry):
        re, im = model[k, 0], model[k, 1]
        acc = []
        for e in range(4):
            x, y = out_ref[0, e], out_ref[1, e]
            acc.append((jnp.sum(re * x + im * y, axis=0, keepdims=True), jnp.sum(re * y - im * x, axis=0, keepdims=True)))
        power = jnp.sum(re * re + im * im, axis=0, keepdims=True)
        first, second = jones(k, 0), jones(k, 1)
        for side, (grad, other) in enumerate(((product(acc, second), second), (product(adjoint(acc), first), first))):
            norm = None
            for x, y in other:
                norm = x * x + y * y if norm is None else norm + (x * x + y * y)
            rows = [-grad[e][0] for e in range(4)] + [-grad[e][1] for e in range(4)] + [power * norm]
            left[side, pl.ds(pl.multiple_of(16 * k, 16), 16), :] = jnp.concatenate(
                rows + [jnp.zeros((7, width), jnp.float32)], axis=0)
        return carry

    lax.fori_loop(0, facets, terms, 0)
    sums = None
    for side in range(2):
        term = exact_dot(left[side], hot[side], ((1,), (1,)))
        sums = term if sums is None else sums + term
    for k in range(facets):
        for r in range(ROWS):
            for g in range(groups):
                parts[k, r, g : g + 1, :] = sums[16 * k + r : 16 * k + r + 1, g * LANES : (g + 1) * LANES]
    value = parts[me]
    copies = []
    for s, (phase, inbox) in enumerate(zip(phases, inboxes)):
        if s > 0:
            mine[s - 1] = value
        before = len(copies)
        for d, peer in enumerate(phase):
            message = pltpu.make_async_remote_copy(
                src_ref=parts.at[peer[1]] if s == 0 else mine.at[s - 1], dst_ref=inbox.at[d],
                send_sem=send_sem.at[before + d], recv_sem=recv_sem.at[before + d], device_id=peer, device_id_type=MESH)
            message.start()
            copies.append(message)
        for message in copies[before:]:
            message.wait_recv()
        for d in range(len(phase)):
            value = value + inbox[d]
    totals_ref[...] = value
    for message in copies + shares:
        message.wait_send()


def body(blocks, facets, observed, station_pairs, station_uvw, directions, fluxes, counts, jones_gains):
    f32 = jnp.float32
    stations = jones_gains.shape[3]
    cap = fluxes.shape[1]
    samples = observed.shape[2]
    share = observed.shape[3] // facets
    vmem = pl.BlockSpec(memory_space=VMEM)
    smem = pl.BlockSpec(memory_space=SMEM)
    facet = lax.axis_index("facet")
    width = -(-share // LANES) * LANES
    sliced = width == share
    if not sliced:
        pad = width - share
        observed = lax.dynamic_slice_in_dim(observed, facet * share, share, 3)
        station_pairs = lax.dynamic_slice_in_dim(station_pairs, facet * share, share, 1)
        observed = jnp.pad(observed, ((0, 0),) * 3 + ((0, pad),))
        station_pairs = jnp.pad(station_pairs, ((0, 0), (0, pad)), constant_values=-1)
    tile = (ROWS, stations // LANES, LANES)
    messages = message_counts(blocks, facets)
    dma = pltpu.SemaphoreType.DMA
    residual, totals = pl.pallas_call(
        functools.partial(calibrate_kernel, blocks, facets, sliced),
        out_shape=(jax.ShapeDtypeStruct((2, 4, samples, width), f32), jax.ShapeDtypeStruct(tile, f32)),
        in_specs=[pl.BlockSpec(memory_space=pl.ANY), vmem, vmem, vmem, vmem, smem, vmem],
        out_specs=(vmem, vmem),
        scratch_shapes=[
            pltpu.VMEM((facets, 16, stations), f32),
            pltpu.VMEM((40, stations), f32),
            pltpu.VMEM((2, 32 + 8 * facets, width), f32),
            pltpu.VMEM((2, stations, width), jnp.bfloat16),
            pltpu.VMEM((8, (TIMES + 1) * width), f32),
            pltpu.VMEM((cap, (TIMES + 1) * width), f32),
            pltpu.VMEM((facets, 2, samples, width), f32),
            pltpu.VMEM((2, 16 * facets, width), f32),
            pltpu.VMEM((facets,) + tile, f32),
            pltpu.VMEM((max(len(messages) - 1, 1),) + tile, f32),
        ]
        + [pltpu.VMEM((n,) + tile, f32) for n in messages]
        + [dma, dma((facets - 1,)), dma((facets - 1,)), dma((sum(messages),)), dma((sum(messages),))],
        compiler_params=pltpu.CompilerParams(collective_id=0, has_side_effects=True),
        name="calibrate",
    )(observed, station_pairs, jnp.transpose(station_uvw, (1, 0, 2)), directions, fluxes, counts, jones_gains)
    if not sliced:
        residual = residual[..., :share]
    scaled = (totals[: ROWS - 1] / (jnp.sqrt(totals[ROWS - 1 :]) + 1.0)).reshape(2, 4, 1, stations)
    return residual, scaled


def solution(mesh):
    placed = (
        P(None, None, None, "base"),
        P(None, "base"),
        P(),
        P("facet", None, None),
        P("facet", None),
        P("facet"),
        P(None, None, "facet", None),
    )
    return jax.shard_map(
        functools.partial(body, mesh.shape["base"], mesh.shape["facet"]),
        mesh=mesh,
        in_specs=placed,
        out_specs=(P(None, None, None, ("base", "facet")), P(None, None, "facet", None)),
        check_vma=False,
    )
```

profile of v0, /device:TPU:0, one launch (start us, length us, event | category | flops | bytes accessed | tf_op | source)
XLA Modules:
  0.0 29.3 jit_solution(4761088065666545393)
XLA Ops:
  1.3 24.3 %calibrate.1 = (f32[2,4,64,128]{3,2,1,0:T(8,128)}, f32[9,4,128]{2,1,0:T(4,128)}) custom-call(f32[2,4,64,256]{3,2,1,0:T(8,128)} %observed_ref.1, s32[2,256]{1,0:T(2,128)} %pairs_ref.1, f32[3,4,512]{2,1,0:T(4,128)} %bitcast.4, f32[1,2,256]{2,1,0:T(2,128)} %directions_ref.1, f32[1,256]{1,0:T(1,128)} %fluxes_ref.1, s32[1]{0:T(128)S(6)} %copy.11.counts_ref, ...), custom_call_target="tpu_custom_call" | custom-call | tf_op jit(solution)/shard_map/calibrate/pallas_call | solution.py:292
  25.6 0.7 %add_bitcast_fusion = f32[4,128]{1,0:T(4,128)S(1)} fusion(f32[9,4,128]{2,1,0:T(4,128)} %get-tuple-element.5), kind=kLoop, calls=%fused_computation.1 | loop fusion | flops 512 | bytes 4096 | tf_op jit(solution)/shard_map/div | solution.py:316
  26.3 1.3 %slice_divide_fusion = f32[8,4,128]{2,1,0:T(4,128)} fusion(f32[9,4,128]{2,1,0:T(4,128)} %get-tuple-element.5, f32[4,128]{1,0:T(4,128)S(1)} %add_bitcast_fusion), kind=kLoop, calls=%fused_computation | loop fusion | flops 4096 | bytes 34816 | tf_op jit(solution)/shard_map/div | solution.py:316
  27.6 1.7 %copy.12 = f32[2,4,64,128]{3,2,1,0:T(8,128)} copy(f32[2,4,64,128]{3,2,1,0:T(8,128)} %get-tuple-element.10) | data formatting | bytes 524288
where the time goes:
time: 29.6 us; the launch traced here: 29.3 us
  Pallas kernels  24.3 us (82%)
  other arithmetic  2.02 us (7%)
  local copies, waits for them, and re-layouts  1.67 us (6%)
  between operations  1.29 us (4%)
    pallas_call x1, Pallas kernels, body(): pl.pallas_call(functools.partial(calibrate_kernel, blocks, facets, sliced...  24.3 us
    div x2, other arithmetic, body(): totals[:ROWS - 1] / (jnp.sqrt(totals[ROWS - 1:]) + 1.0)  2.02 us
    unnamed x1, local copies, waits for them, and re-layouts  1.67 us

commit v1 on v0

--- a/solution.py
+++ b/solution.py
@@ -46,11 +46,9 @@
 
 
 def exact_dot(a, hot, dims):
-    out = None
-    for part in split3(a):
-        term = lax.dot_general(part, hot, (dims, ((), ())), preferred_element_type=jnp.float32)
-        out = term if out is None else out + term
-    return out
+    rows = a.shape[0]
+    out = lax.dot_general(jnp.concatenate(split3(a), axis=0), hot, (dims, ((), ())), preferred_element_type=jnp.float32)
+    return out[:rows] + out[rows : 2 * rows] + out[2 * rows :]
 
 
 def product(a, b):
@@ -98,11 +96,11 @@
 
 
 def calibrate_kernel(blocks, facets, sliced, observed_ref, pairs_ref, uvw_ref, directions_ref, fluxes_ref, counts_ref,
-                     gains_ref, out_ref, totals_ref, params, table, gathered, hot, base, angle, model, left, parts, mine,
+                     gains_ref, residual_ref, totals_ref, out_ref, params, table, gathered, hot, base, angle, model, left, parts, mine,
                      *refs):
     phases = partners(blocks, facets)
     inboxes = refs[: len(phases)]
-    copy_sem, params_send, params_recv, send_sem, recv_sem = refs[len(phases) :]
+    copy_sem, out_sem, params_send, params_recv, send_sem, recv_sem = refs[len(phases) :]
     me = lax.axis_index("facet")
     block = lax.axis_index("base")
     barrier = pltpu.get_barrier_semaphore()
@@ -144,7 +142,7 @@
         for axis in range(3):
             table[8 * t + axis : 8 * t + axis + 1, :] = uvw_ref[axis, t : t + 1, :]
         table[8 * t + 3 : 8 * t + 8, :] = jnp.zeros((5, stations), jnp.float32)
-    table[32:40, :] = params[me, 0:8, :]
+    table[32:48, :] = params[me]
     own = pl.ds(pl.multiple_of(32 + 8 * me, 8), 8)
     for side in range(2):
         found = exact_dot(table[...], hot[side], ((1,), (0,)))
@@ -152,8 +150,6 @@
         gathered[side, own, :] = found[32:40]
     for t in range(TIMES):
         base[:, t * width : (t + 1) * width] = gathered[0, 8 * t : 8 * t + 8, :] - gathered[1, 8 * t : 8 * t + 8, :]
-    row = lax.broadcasted_iota(jnp.int32, (8, width), 0)
-    base[:, TIMES * width :] = (row == 3).astype(jnp.float32)
 
     def jones(k, side):
         rows = gathered[side, pl.ds(pl.multiple_of(32 + 8 * k, 8), 8), :]
@@ -162,13 +158,15 @@
     def facet_model(d, carry):
         k = lax.rem(me + d, facets)
         slots = jnp.transpose(params[k, 8:16, 0:cap])
-        angle[...] = jnp.dot(slots, base[...], precision=lax.Precision.HIGHEST, preferred_element_type=jnp.float32)
+        for v in range(4):
+            angle[v] = jnp.broadcast_to(slots[:, v : v + 1], (cap, width))
         for t in range(TIMES):
-
-            def step(i, acc):
+            u, v, w = (jnp.broadcast_to(base[c : c + 1, t * width : (t + 1) * width], (STEP, width)) for c in range(3))
+
+            def step(i, acc, u=u, v=v, w=w):
                 rows = pl.ds(pl.multiple_of(i * STEP, STEP), STEP)
-                turns = angle[rows, t * width : (t + 1) * width]
-                live = angle[rows, TIMES * width :]
+                turns = u * angle[0, rows, :] + v * angle[1, rows, :] + w * angle[2, rows, :]
+                live = angle[3, rows, :]
                 cz, sz = cos_sin_turns(turns * (79.0 / 64.0))
                 c0, s0 = cos_sin_turns(turns * (1.0 / 64.0))
                 cz, sz = cz * live, sz * live
@@ -189,7 +187,7 @@
                 return tuple(out)
 
             zero = jnp.zeros((8, width), jnp.float32)
-            acc = lax.fori_loop(0, cap // STEP, step, (zero,) * 32)
+            acc = lax.fori_loop(0, cap // STEP, step, (zero,) * 32, unroll=4)
             real, imaginary = [None] * CHANNELS, [None] * CHANNELS
             for centre in range(2):
                 for j in range(4):
@@ -208,7 +206,7 @@
         pltpu.make_async_copy(params.at[other], params.at[other], params_recv.at[d - 1]).wait()
         rows = pl.ds(pl.multiple_of(32 + 8 * other, 8), 8)
         for side in range(2):
-            gathered[side, rows, :] = exact_dot(params[other, 0:8, :], hot[side], ((1,), (0,)))
+            gathered[side, rows, :] = exact_dot(params[other], hot[side], ((1,), (0,)))[0:8]
     lax.fori_loop(1, facets, facet_model, 0)
     copy.wait()
 
@@ -221,6 +219,8 @@
         return carry
 
     lax.fori_loop(0, facets, subtract, 0)
+    written = pltpu.make_async_copy(out_ref, residual_ref, out_sem)
+    written.start()
 
     def terms(k, carry):
         re, im = model[k, 0], model[k, 1]
@@ -267,6 +267,18 @@
     totals_ref[...] = value
     for message in copies + shares:
         message.wait_send()
+    written.wait()
+
+
+def finish_kernel(totals_ref, residual_ref, scaled_ref, out_ref, copy_sem):
+    copy = pltpu.make_async_copy(residual_ref, out_ref, copy_sem)
+    copy.start()
+    scale = 1.0 / (jnp.sqrt(totals_ref[ROWS - 1]) + 1.0)
+    for r in range(ROWS - 1):
+        value = totals_ref[r] * scale
+        for g in range(value.shape[0]):
+            scaled_ref[r // 4, r % 4, 0:1, g * LANES : (g + 1) * LANES] = value[g : g + 1, :]
+    copy.wait()
 
 
 def body(blocks, facets, observed, station_pairs, station_uvw, directions, fluxes, counts, jones_gains):
@@ -293,27 +305,36 @@
         functools.partial(calibrate_kernel, blocks, facets, sliced),
         out_shape=(jax.ShapeDtypeStruct((2, 4, samples, width), f32), jax.ShapeDtypeStruct(tile, f32)),
         in_specs=[pl.BlockSpec(memory_space=pl.ANY), vmem, vmem, vmem, vmem, smem, vmem],
-        out_specs=(vmem, vmem),
+        out_specs=(pl.BlockSpec(memory_space=pl.ANY), vmem),
         scratch_shapes=[
+            pltpu.VMEM((2, 4, samples, width), f32),
             pltpu.VMEM((facets, 16, stations), f32),
-            pltpu.VMEM((40, stations), f32),
+            pltpu.VMEM((48, stations), f32),
             pltpu.VMEM((2, 32 + 8 * facets, width), f32),
             pltpu.VMEM((2, stations, width), jnp.bfloat16),
-            pltpu.VMEM((8, (TIMES + 1) * width), f32),
-            pltpu.VMEM((cap, (TIMES + 1) * width), f32),
+            pltpu.VMEM((8, TIMES * width), f32),
+            pltpu.VMEM((4, cap, width), f32),
             pltpu.VMEM((facets, 2, samples, width), f32),
             pltpu.VMEM((2, 16 * facets, width), f32),
             pltpu.VMEM((facets,) + tile, f32),
             pltpu.VMEM((max(len(messages) - 1, 1),) + tile, f32),
         ]
         + [pltpu.VMEM((n,) + tile, f32) for n in messages]
-        + [dma, dma((facets - 1,)), dma((facets - 1,)), dma((sum(messages),)), dma((sum(messages),))],
+        + [dma, dma, dma((facets - 1,)), dma((facets - 1,)), dma((sum(messages),)), dma((sum(messages),))],
         compiler_params=pltpu.CompilerParams(collective_id=0, has_side_effects=True),
         name="calibrate",
     )(observed, station_pairs, jnp.transpose(station_uvw, (1, 0, 2)), directions, fluxes, counts, jones_gains)
+    anywhere = pl.BlockSpec(memory_space=pl.ANY)
+    scaled, residual = pl.pallas_call(
+        finish_kernel,
+        out_shape=(jax.ShapeDtypeStruct((2, 4, 1, stations), f32), jax.ShapeDtypeStruct(residual.shape, f32)),
+        in_specs=[vmem, anywhere],
+        out_specs=(vmem, vmem),
+        scratch_shapes=[dma],
+        name="finish",
+    )(totals, residual)
     if not sliced:
         residual = residual[..., :share]
-    scaled = (totals[: ROWS - 1] / (jnp.sqrt(totals[ROWS - 1 :]) + 1.0)).reshape(2, 4, 1, stations)
     return residual, scaled
 
 

time: 29.6 us -> 25 us (0.84)
  other arithmetic: 2.02 us -> 0 us
  local copies, waits for them, and re-layouts: 1.67 us -> 0 us
  Pallas kernels: 24.3 us -> 23.4 us
    pallas_call x1, Pallas kernels: 24.3 us -> 21 us  [body(): pl.pallas_call(functools.partial(calibrate_kernel, blocks, facets, sliced...]
    pallas_call x0 -> x1, Pallas kernels: none -> 2.39 us  [body(): pl.pallas_call(finish_kernel, out_shape=(jax.ShapeDtypeStruct((2, 4, 1, s...]
    div x2 -> x0, other arithmetic: 2.02 us -> none  [body(): totals[:ROWS - 1] / (jnp.sqrt(totals[ROWS - 1:]) + 1.0)]
    unnamed x1 -> x0, local copies, waits for them, and re-layouts: 1.67 us -> none
where the time goes in v1:
time: 25 us; the launch traced here: 24.7 us
  Pallas kernels  23.4 us (94%)
  between operations  1.29 us (5%)
    pallas_call x1, Pallas kernels, body(): pl.pallas_call(functools.partial(calibrate_kernel, blocks, facets, sliced...  21 us
    pallas_call x1, Pallas kernels, body(): pl.pallas_call(finish_kernel, out_shape=(jax.ShapeDtypeStruct((2, 4, 1, s...  2.39 us

profile of v1, /device:TPU:0, one launch (start us, length us, event | category | flops | bytes accessed | tf_op | source)
XLA Modules:
  0.0 24.7 jit_solution(12682580175666375790)
XLA Ops:
  1.3 21.0 %calibrate.1 = (f32[2,4,64,128]{3,2,1,0:T(8,128)}, f32[9,4,128]{2,1,0:T(4,128)}) custom-call(f32[2,4,64,256]{3,2,1,0:T(8,128)} %observed_ref.1, s32[2,256]{1,0:T(2,128)} %pairs_ref.1, f32[3,4,512]{2,1,0:T(4,128)} %bitcast.1, f32[1,2,256]{2,1,0:T(2,128)} %directions_ref.1, f32[1,256]{1,0:T(1,128)} %fluxes_ref.1, s32[1]{0:T(128)S(6)} %copy.9.counts_ref, ...), custom_call_target="tpu_custom_call" | custom-call | tf_op jit(solution)/shard_map/calibrate/pallas_call | solution.py:304
  22.3 2.4 %finish.1 = (f32[2,4,1,512]{3,2,1,0:T(1,128)}, f32[2,4,64,128]{3,2,1,0:T(8,128)}) custom-call(f32[9,4,128]{2,1,0:T(4,128)} %get-tuple-element.6.totals_ref, f32[2,4,64,128]{3,2,1,0:T(8,128)} %get-tuple-element.7.residual_ref), custom_call_target="tpu_custom_call" | custom-call | tf_op jit(solution)/shard_map/finish/pallas_call | solution.py:328

commit v2 on v1

--- a/solution.py
+++ b/solution.py
@@ -187,7 +187,7 @@
                 return tuple(out)
 
             zero = jnp.zeros((8, width), jnp.float32)
-            acc = lax.fori_loop(0, cap // STEP, step, (zero,) * 32, unroll=4)
+            acc = lax.fori_loop(0, cap // STEP, step, (zero,) * 32, unroll=8)
             real, imaginary = [None] * CHANNELS, [None] * CHANNELS
             for centre in range(2):
                 for j in range(4):
@@ -218,7 +218,7 @@
             out_ref[1, e] = out_ref[1, e] - (re * y + im * x)
         return carry
 
-    lax.fori_loop(0, facets, subtract, 0)
+    lax.fori_loop(0, facets, subtract, 0, unroll=2)
     written = pltpu.make_async_copy(out_ref, residual_ref, out_sem)
     written.start()
 
@@ -239,7 +239,7 @@
                 rows + [jnp.zeros((7, width), jnp.float32)], axis=0)
         return carry
 
-    lax.fori_loop(0, facets, terms, 0)
+    lax.fori_loop(0, facets, terms, 0, unroll=2)
     sums = None
     for side in range(2):
         term = exact_dot(left[side], hot[side], ((1,), (1,)))

time: 25 us -> 24.7 us (0.988)
    pallas_call x1, Pallas kernels: 21 us -> 20.8 us  [body(): pl.pallas_call(functools.partial(calibrate_kernel, blocks, facets, sliced...]
where the time goes in v2:
time: 24.7 us; the launch traced here: 24.5 us
  Pallas kernels  23.2 us (94%)
  between operations  1.29 us (5%)
    pallas_call x1, Pallas kernels, body(): pl.pallas_call(functools.partial(calibrate_kernel, blocks, facets, sliced...  20.8 us
    pallas_call x1, Pallas kernels, body(): pl.pallas_call(finish_kernel, out_shape=(jax.ShapeDtypeStruct((2, 4, 1, s...  2.39 us

profile of v2, /device:TPU:0, one launch (start us, length us, event | category | flops | bytes accessed | tf_op | source)
XLA Modules:
  0.0 24.5 jit_solution(8655652640589136949)
XLA Ops:
  1.3 20.8 %calibrate.1 = (f32[2,4,64,128]{3,2,1,0:T(8,128)}, f32[9,4,128]{2,1,0:T(4,128)}) custom-call(f32[2,4,64,256]{3,2,1,0:T(8,128)} %observed_ref.1, s32[2,256]{1,0:T(2,128)} %pairs_ref.1, f32[3,4,512]{2,1,0:T(4,128)} %bitcast.1, f32[1,2,256]{2,1,0:T(2,128)} %directions_ref.1, f32[1,256]{1,0:T(1,128)} %fluxes_ref.1, s32[1]{0:T(128)S(6)} %copy.9.counts_ref, ...), custom_call_target="tpu_custom_call" | custom-call | tf_op jit(solution)/shard_map/calibrate/pallas_call | solution.py:304
  22.1 2.4 %finish.1 = (f32[2,4,1,512]{3,2,1,0:T(1,128)}, f32[2,4,64,128]{3,2,1,0:T(8,128)}) custom-call(f32[9,4,128]{2,1,0:T(4,128)} %get-tuple-element.6.totals_ref, f32[2,4,64,128]{3,2,1,0:T(8,128)} %get-tuple-element.7.residual_ref), custom_call_target="tpu_custom_call" | custom-call | tf_op jit(solution)/shard_map/finish/pallas_call | solution.py:328
